TPU v7x, 32 devices: a whole 2x2x4 slice. The times are simulated.
32 devices in a mesh: pb: 4 (over y, x), item: 8 (over z, core).
Axes of the slice: x: 2, y: 2, z: 4, core: 2. Of those that a mesh axis runs over, the one named last changes fastest.
Arguments:
- queries: bfloat16 [2048, 512], P(('pb', 'item')), may hold values from -2 to 2
- gate_query: bfloat16 [2048, 64], P(('pb', 'item')), may hold values from -6 to 250
- items: bfloat16 [4096, 512], P(('item', 'pb')), may hold values from -2 to 2
- gate_items: bfloat16 [4096, 64], P(('item', 'pb')), may hold values from -6 to 6
- slot_tiles: int32 [4, 48], P('pb', 'item'), may hold values from -1 to 15, as said below
- d_scores: bfloat16 [4, 48, 128, 128], P('pb', 'item'), may hold values from -6 to 6
Outputs:
- grad_queries: bfloat16 [2048, 512], P(('pb', 'item'))
- grad_gate_query: float32 [2048, 64], P(('pb', 'item'))
- grad_items: bfloat16 [4096, 512], P(('item', 'pb'))
- grad_gate_items: float32 [4096, 64], P(('item', 'pb'))
Inputs may be any that keep to these rules, and one draw needn't show every extreme that they name: `slot_tiles`: each device's row of slots names distinct tiles, live ones first and -1 after them. Devices (p, j) and (p, j + 8 / 2) form a pair: either one of them has all 6 slots live and the other exactly one, or both have between 1 and 3 live slots. Device (0, 0) has all 6 live.
All inputs are finite; a program needn't handle non-finite values.
Results may differ from a plain program's by a relative error of at most 0.0049.
Values may be sent and summed in bfloat16 or wider, within the bound.
A program may use at most 64 MiB of HBM per device.

v0:
```python
import jax
import jax.numpy as jnp
from jax import lax
from jax.sharding import PartitionSpec as P

E = 64
KQ = 8
KI = 8


def tile_grads(query_tile, query_gate, item_tile, item_gate, cotangent):
    extent = query_tile.shape[0]
    query_parts = query_tile.reshape(extent, KQ, E)
    item_parts = item_tile.reshape(extent, KI, E)
    logits = jnp.einsum(
        "qae,ibe->abqi", query_parts, item_parts, preferred_element_type=jnp.float32
    ).reshape(KQ * KI, extent, extent)
    gates = (
        query_gate.astype(jnp.float32).T[:, :, None] + item_gate.astype(jnp.float32).T[:, None, :]
    )
    weights = jax.nn.softmax(gates, axis=0)
    score = jnp.sum(weights * logits, axis=0)
    upstream = cotangent.astype(jnp.float32)[None]
    logit_grad = (upstream * weights).astype(jnp.bfloat16)
    gate_grad = upstream * weights * (logits - score[None])
    logit_parts = logit_grad.reshape(KQ, KI, extent, extent)
    query_grad = jnp.einsum(
        "abqi,ibe->qae", logit_parts, item_parts, preferred_element_type=jnp.float32
    ).reshape(extent, KQ * E)
    item_grad = jnp.einsum(
        "abqi,qae->ibe", logit_parts, query_parts, preferred_element_type=jnp.float32
    ).reshape(extent, KI * E)
    return (query_grad, jnp.sum(gate_grad, axis=2).T, item_grad, jnp.sum(gate_grad, axis=1).T)


def on_device(queries, gate_query, items, gate_items, slot_tiles, d_scores):
    block_queries, block_gates = (
        lax.all_gather(queries, "item", axis=0, tiled=True),
        lax.all_gather(gate_query, "item", axis=0, tiled=True),
    )
    shard_items, shard_gates = (
        lax.all_gather(items, "pb", axis=0, tiled=True),
        lax.all_gather(gate_items, "pb", axis=0, tiled=True),
    )
    extent = d_scores.shape[-1]
    tile_ids = slot_tiles.reshape(-1)
    cotangents = d_scores.reshape(-1, extent, extent)
    slot_count = tile_ids.shape[0]
    item_blocks = shard_items.shape[0] // extent

    def anchors(tile_id):
        safe_id = jnp.maximum(tile_id, 0)
        return (safe_id // item_blocks * extent, safe_id % item_blocks * extent)

    def operands(tile_id):
        query_start, item_start = anchors(tile_id)
        return (
            lax.dynamic_slice_in_dim(block_queries, query_start, extent, 0),
            lax.dynamic_slice_in_dim(block_gates, query_start, extent, 0),
            lax.dynamic_slice_in_dim(shard_items, item_start, extent, 0),
            lax.dynamic_slice_in_dim(shard_gates, item_start, extent, 0),
        )

    def accumulate(current, tile_id, grads):
        query_start, item_start = anchors(tile_id)
        starts = (query_start, query_start, item_start, item_start)
        return tuple(
            (
                lax.dynamic_update_slice_in_dim(
                    total, lax.dynamic_slice_in_dim(total, start, extent, 0) + update, start, 0
                )
                for total, update, start in zip(current, grads, starts)
            )
        )

    totals = (
        jnp.zeros(block_queries.shape, jnp.float32),
        jnp.zeros(block_gates.shape, jnp.float32),
        jnp.zeros(shard_items.shape, jnp.float32),
        jnp.zeros(shard_gates.shape, jnp.float32),
    )

    def home_step(position, current):
        tile_id = tile_ids[position]

        def work(state):
            return accumulate(state, tile_id, tile_grads(*operands(tile_id), cotangents[position]))

        return lax.cond(tile_id >= 0, work, lambda state: state, current)

    totals = lax.fori_loop(0, slot_count, home_step, totals)
    query_sum, query_gate_sum = (
        lax.psum_scatter(totals[0], "item", scatter_dimension=0, tiled=True),
        lax.psum_scatter(totals[1], "item", scatter_dimension=0, tiled=True),
    )
    item_sum, item_gate_sum = (
        lax.psum_scatter(totals[2], "pb", scatter_dimension=0, tiled=True),
        lax.psum_scatter(totals[3], "pb", scatter_dimension=0, tiled=True),
    )
    return (
        query_sum.astype(jnp.bfloat16),
        query_gate_sum,
        item_sum.astype(jnp.bfloat16),
        item_gate_sum,
    )


def solution(mesh):
    return jax.shard_map(
        on_device,
        mesh=mesh,
        in_specs=(
            P(("pb", "item"), None),
            P(("pb", "item"), None),
            P(("item", "pb"), None),
            P(("item", "pb"), None),
            P("pb", "item"),
            P("pb", "item", None, None),
        ),
        out_specs=(
            P(("pb", "item"), None),
            P(("pb", "item"), None),
            P(("item", "pb"), None),
            P(("item", "pb"), None),
        ),
        check_vma=False,
    )
```

profile of v0, /device:TPU:0, one launch (start us, length us, event | category | flops | bytes accessed | tf_op | source)
XLA Modules:
  0.0 288.2 jit_solution(2708447335838776884)
XLA Ops:
  7.2 11.0 %all_gather.14 = bf16[512,64]{0,1:T(8,128)(2,1)} all-gather(bf16[128,64]{0,1:T(8,128)(2,1)} %param.13), channel_id=1, replica_groups=mesh['pb'=4,'item'=8] {'pb'}, dimensions={0}, use_global_device_ids=true | all-gather | bytes 81920 | tf_op jit(solution)/shard_map/all_gather | solution.py:43
  18.3 14.5 %all_gather.13 = bf16[512,64]{1,0:T(8,128)(2,1)S(1)} all-gather(bf16[64,64]{1,0:T(8,128)(2,1)} %param.11), channel_id=1, replica_groups=mesh['pb'=4,'item'=8] {'item'}, dimensions={0}, use_global_device_ids=true | all-gather | bytes 73728 | tf_op jit(solution)/shard_map/all_gather | solution.py:39
  33.9 1.7 copy.59
  35.6 9.6 %all_gather.12 = bf16[512,512]{0,1:T(8,128)(2,1)S(1)} all-gather(bf16[128,512]{0,1:T(8,128)(2,1)S(1)} %copy.58), channel_id=1, replica_groups=mesh['pb'=4,'item'=8] {'pb'}, dimensions={0}, use_global_device_ids=true | all-gather | bytes 655360 | tf_op jit(solution)/shard_map/all_gather | solution.py:42
  45.2 15.0 %all_gather.15 = bf16[512,512]{1,0:T(8,128)(2,1)S(1)} all-gather(bf16[64,512]{1,0:T(8,128)(2,1)} %param.10), channel_id=1, replica_groups=mesh['pb'=4,'item'=8] {'item'}, dimensions={0}, use_global_device_ids=true | all-gather | bytes 589824 | tf_op jit(solution)/shard_map/all_gather | solution.py:38
  62.0 96.5 %while.19 = (s32[]{:T(128)}, f32[512,512]{0,1:T(8,128)S(1)}, f32[512,64]{0,1:T(8,128)}, f32[512,512]{0,1:T(8,128)S(1)}, f32[512,64]{0,1:T(8,128)}, /*index=5*/s3...) while((s32[]{:T(128)}, f32[512,512]{0,1:T(8,128)S(1)}, ...), condition=%wide.region_8.9_spmd, body=%wide.region_0.8_spmd.sunk | while | flops 432128032 | bytes 13894240 | solution.py:91
  63.3 14.8 %conditional.2 = ((f32[512,512]{0,1:T(8,128)S(1)}, f32[512,64]{0,1:T(8,128)}, f32[512,512]{0,1:T(8,128)S(1)}, f32[512,64]{0,1:T(8,128)})) conditional(s32[]{:T(128)} %convert_element_type.27, (f32[512,512]{0,1:T(8,128)S(1)}, f32[512,64]{0,1:T(8,128)}, f32[512,512]{0,1:T(8,128)S(1)}, f32[512,64]{0,1:T(8,128)}) %tuple.50, (s32[]{:T(128)}, ...), branch_computations={%region_1.0_spmd, %region_2.7_spmd} | conditional | flops 432128032 | bytes 13893961 | solution.py:89
  69.6 1.3 fusion.6
  72.4 2.9 %fusion.4 = (f32[8,8,128]{2,0,1:T(8,128)S(1)}, f32[8,8,128]{2,0,1:T(8,128)S(1)}) fusion(f32[128,128]{0,1:T(8,128)S(1)} %get-tuple-element.298, f32[128,8,128,8]{2,0,3,1:T(8,128)S(1)} %get-tuple-element.299, f32[128,128]{0,1:T(8,128)S(1)} %copy.53, f32[128,128]{0,1:T(8,128)S(1)} %copy.52, f32[8,8,128]{2,0,1:T(8,128)S(1)} %copy.51, f32[8,8,128]{2,0,1:T(8,128)S(1)} %copy.50, ...), kind=kLoop, calls=%fused_computation.10 | loop fusion | flops 8372224 | bytes 4587520 | tf_op jit(solution)/shard_map/while/body/eval_jaxpr/cond/branch_1_fun/reduce_sum | solution.py:33
  75.3 1.4 fusion.8
  76.7 1.4 fusion.9
  79.3 14.8 %conditional.2 = ((f32[512,512]{0,1:T(8,128)S(1)}, f32[512,64]{0,1:T(8,128)}, f32[512,512]{0,1:T(8,128)S(1)}, f32[512,64]{0,1:T(8,128)})) conditional(s32[]{:T(128)} %convert_element_type.27, (f32[512,512]{0,1:T(8,128)S(1)}, f32[512,64]{0,1:T(8,128)}, f32[512,512]{0,1:T(8,128)S(1)}, f32[512,64]{0,1:T(8,128)}) %tuple.50, (s32[]{:T(128)}, ...), branch_computations={%region_1.0_spmd, %region_2.7_spmd} | conditional | flops 432128032 | bytes 13893961 | solution.py:89
  84.3 1.3 fusion.7
  85.6 1.3 fusion.6
  88.5 2.9 %fusion.4 = (f32[8,8,128]{2,0,1:T(8,128)S(1)}, f32[8,8,128]{2,0,1:T(8,128)S(1)}) fusion(f32[128,128]{0,1:T(8,128)S(1)} %get-tuple-element.298, f32[128,8,128,8]{2,0,3,1:T(8,128)S(1)} %get-tuple-element.299, f32[128,128]{0,1:T(8,128)S(1)} %copy.53, f32[128,128]{0,1:T(8,128)S(1)} %copy.52, f32[8,8,128]{2,0,1:T(8,128)S(1)} %copy.51, f32[8,8,128]{2,0,1:T(8,128)S(1)} %copy.50, ...), kind=kLoop, calls=%fused_computation.10 | loop fusion | flops 8372224 | bytes 4587520 | tf_op jit(solution)/shard_map/while/body/eval_jaxpr/cond/branch_1_fun/reduce_sum | solution.py:33
  91.4 1.4 fusion.8
  92.8 1.4 fusion.9
  95.4 14.8 %conditional.2 = ((f32[512,512]{0,1:T(8,128)S(1)}, f32[512,64]{0,1:T(8,128)}, f32[512,512]{0,1:T(8,128)S(1)}, f32[512,64]{0,1:T(8,128)})) conditional(s32[]{:T(128)} %convert_element_type.27, (f32[512,512]{0,1:T(8,128)S(1)}, f32[512,64]{0,1:T(8,128)}, f32[512,512]{0,1:T(8,128)S(1)}, f32[512,64]{0,1:T(8,128)}) %tuple.50, (s32[]{:T(128)}, ...), branch_computations={%region_1.0_spmd, %region_2.7_spmd} | conditional | flops 432128032 | bytes 13893961 | solution.py:89
  101.7 1.3 fusion.6
  104.5 2.9 %fusion.4 = (f32[8,8,128]{2,0,1:T(8,128)S(1)}, f32[8,8,128]{2,0,1:T(8,128)S(1)}) fusion(f32[128,128]{0,1:T(8,128)S(1)} %get-tuple-element.298, f32[128,8,128,8]{2,0,3,1:T(8,128)S(1)} %get-tuple-element.299, f32[128,128]{0,1:T(8,128)S(1)} %copy.53, f32[128,128]{0,1:T(8,128)S(1)} %copy.52, f32[8,8,128]{2,0,1:T(8,128)S(1)} %copy.51, f32[8,8,128]{2,0,1:T(8,128)S(1)} %copy.50, ...), kind=kLoop, calls=%fused_computation.10 | loop fusion | flops 8372224 | bytes 4587520 | tf_op jit(solution)/shard_map/while/body/eval_jaxpr/cond/branch_1_fun/reduce_sum | solution.py:33
  107.5 1.4 fusion.8
  108.9 1.4 fusion.9
  111.5 14.8 %conditional.2 = ((f32[512,512]{0,1:T(8,128)S(1)}, f32[512,64]{0,1:T(8,128)}, f32[512,512]{0,1:T(8,128)S(1)}, f32[512,64]{0,1:T(8,128)})) conditional(s32[]{:T(128)} %convert_element_type.27, (f32[512,512]{0,1:T(8,128)S(1)}, f32[512,64]{0,1:T(8,128)}, f32[512,512]{0,1:T(8,128)S(1)}, f32[512,64]{0,1:T(8,128)}) %tuple.50, (s32[]{:T(128)}, ...), branch_computations={%region_1.0_spmd, %region_2.7_spmd} | conditional | flops 432128032 | bytes 13893961 | solution.py:89
  116.5 1.3 fusion.7
  117.8 1.3 fusion.6
  120.6 2.9 %fusion.4 = (f32[8,8,128]{2,0,1:T(8,128)S(1)}, f32[8,8,128]{2,0,1:T(8,128)S(1)}) fusion(f32[128,128]{0,1:T(8,128)S(1)} %get-tuple-element.298, f32[128,8,128,8]{2,0,3,1:T(8,128)S(1)} %get-tuple-element.299, f32[128,128]{0,1:T(8,128)S(1)} %copy.53, f32[128,128]{0,1:T(8,128)S(1)} %copy.52, f32[8,8,128]{2,0,1:T(8,128)S(1)} %copy.51, f32[8,8,128]{2,0,1:T(8,128)S(1)} %copy.50, ...), kind=kLoop, calls=%fused_computation.10 | loop fusion | flops 8372224 | bytes 4587520 | tf_op jit(solution)/shard_map/while/body/eval_jaxpr/cond/branch_1_fun/reduce_sum | solution.py:33
  123.5 1.4 fusion.8
  124.9 1.4 fusion.9
  127.5 14.8 %conditional.2 = ((f32[512,512]{0,1:T(8,128)S(1)}, f32[512,64]{0,1:T(8,128)}, f32[512,512]{0,1:T(8,128)S(1)}, f32[512,64]{0,1:T(8,128)})) conditional(s32[]{:T(128)} %convert_element_type.27, (f32[512,512]{0,1:T(8,128)S(1)}, f32[512,64]{0,1:T(8,128)}, f32[512,512]{0,1:T(8,128)S(1)}, f32[512,64]{0,1:T(8,128)}) %tuple.50, (s32[]{:T(128)}, ...), branch_computations={%region_1.0_spmd, %region_2.7_spmd} | conditional | flops 432128032 | bytes 13893961 | solution.py:89
  132.5 1.3 fusion.7
  133.9 1.3 fusion.6
  136.7 2.9 %fusion.4 = (f32[8,8,128]{2,0,1:T(8,128)S(1)}, f32[8,8,128]{2,0,1:T(8,128)S(1)}) fusion(f32[128,128]{0,1:T(8,128)S(1)} %get-tuple-element.298, f32[128,8,128,8]{2,0,3,1:T(8,128)S(1)} %get-tuple-element.299, f32[128,128]{0,1:T(8,128)S(1)} %copy.53, f32[128,128]{0,1:T(8,128)S(1)} %copy.52, f32[8,8,128]{2,0,1:T(8,128)S(1)} %copy.51, f32[8,8,128]{2,0,1:T(8,128)S(1)} %copy.50, ...), kind=kLoop, calls=%fused_computation.10 | loop fusion | flops 8372224 | bytes 4587520 | tf_op jit(solution)/shard_map/while/body/eval_jaxpr/cond/branch_1_fun/reduce_sum | solution.py:33
  139.6 1.4 fusion.8
  141.0 1.4 fusion.9
  143.6 14.9 %conditional.2 = ((f32[512,512]{0,1:T(8,128)S(1)}, f32[512,64]{0,1:T(8,128)}, f32[512,512]{0,1:T(8,128)S(1)}, f32[512,64]{0,1:T(8,128)})) conditional(s32[]{:T(128)} %convert_element_type.27, (f32[512,512]{0,1:T(8,128)S(1)}, f32[512,64]{0,1:T(8,128)}, f32[512,512]{0,1:T(8,128)S(1)}, f32[512,64]{0,1:T(8,128)}) %tuple.50, (s32[]{:T(128)}, ...), branch_computations={%region_1.0_spmd, %region_2.7_spmd} | conditional | flops 432128032 | bytes 13893961 | solution.py:89
  148.6 1.3 fusion.7
  149.9 1.3 fusion.6
  152.8 2.9 %fusion.4 = (f32[8,8,128]{2,0,1:T(8,128)S(1)}, f32[8,8,128]{2,0,1:T(8,128)S(1)}) fusion(f32[128,128]{0,1:T(8,128)S(1)} %get-tuple-element.298, f32[128,8,128,8]{2,0,3,1:T(8,128)S(1)} %get-tuple-element.299, f32[128,128]{0,1:T(8,128)S(1)} %copy.53, f32[128,128]{0,1:T(8,128)S(1)} %copy.52, f32[8,8,128]{2,0,1:T(8,128)S(1)} %copy.51, f32[8,8,128]{2,0,1:T(8,128)S(1)} %copy.50, ...), kind=kLoop, calls=%fused_computation.10 | loop fusion | flops 8372224 | bytes 4587520 | tf_op jit(solution)/shard_map/while/body/eval_jaxpr/cond/branch_1_fun/reduce_sum | solution.py:33
  155.7 1.4 fusion.8
  157.1 1.4 fusion.9
  159.9 1.4 copy.64
  162.1 1.8 copy.63
  163.8 28.4 %reduce-scatter.5.cloned.1.call-done = f32[64,512]{1,0:T(8,128)} async-done(((f32[512,512]{1,0:T(8,128)}), f32[64,512]{1,0:T(8,128)}) %reduce-scatter.5.cloned.1.call-update) | async-done | bytes 131088 | tf_op jit(solution)/shard_map/reduce_scatter | solution.py:93
  192.3 1.5 convert_element_type.21
  193.8 27.4 %reduce-scatter.9.cloned.1.call-done = f32[128,512]{1,0:T(8,128)} async-done(((f32[512,512]{1,0:T(8,128)}), f32[128,512]{1,0:T(8,128)}) %reduce-scatter.9.cloned.1.call-update) | async-done | bytes 262160 | tf_op jit(solution)/shard_map/reduce_scatter | solution.py:97
  221.2 1.6 convert_element_type.22
  222.8 25.8 %reduce-scatter.11.cloned.1.call-done = f32[128,64]{0,1:T(8,128)} async-done(((f32[512,64]{0,1:T(8,128)}), f32[128,64]{0,1:T(8,128)}) %reduce-scatter.11.cloned.1.call-update) | async-done | bytes 32784 | tf_op jit(solution)/shard_map/reduce_scatter | solution.py:98
  248.6 33.1 %reduce-scatter.7.cloned.1.call-done = f32[64,64]{1,0:T(8,128)} async-done(((f32[512,64]{1,0:T(8,128)}), f32[64,64]{1,0:T(8,128)}) %reduce-scatter.7.cloned.1.call-update) | async-done | bytes 16400 | tf_op jit(solution)/shard_map/reduce_scatter | solution.py:94
  (98 shorter events, 45.4 us)
Async XLA Ops:
  7.2 54.8 %copy-start = (s32[1,6]{1,0:T(1,128)S(1)}, s32[1,6]{1,0:T(1,128)}, u32[]{:S(2)}) copy-start(s32[1,6]{1,0:T(1,128)} %param.14) | copy-start | bytes 76
  7.2 185.1 %reduce-scatter.5.cloned.1.call-start = ((), (), s32[]{:S(2)}) async-start(), calls=%async_computation.4 | async-start | bytes 1179648 | tf_op jit(solution)/shard_map/reduce_scatter | solution.py:93
  159.8 61.4 %reduce-scatter.9.cloned.1.call-start = ((), (), s32[]{:S(2)}) async-start(), calls=%async_computation.6 | async-start | bytes 1310720 | tf_op jit(solution)/shard_map/reduce_scatter | solution.py:97
  161.3 87.3 %reduce-scatter.11.cloned.1.call-start = ((), (), s32[]{:S(2)}) async-start(), calls=%async_computation.7 | async-start | bytes 163840 | tf_op jit(solution)/shard_map/reduce_scatter | solution.py:98
  162.0 119.7 %reduce-scatter.7.cloned.1.call-start = ((), (), s32[]{:S(2)}) async-start(), calls=%async_computation.5 | async-start | bytes 294912 | tf_op jit(solution)/shard_map/reduce_scatter | solution.py:94
Sparse Core Ops, SparseCore 0:
  159.9 32.2 reduce-scatter.4
  195.2 25.9 reduce-scatter.8
  224.7 23.8 reduce-scatter.10
  251.3 30.3 reduce-scatter.6
where the time goes:
time: 289 us; the launch traced here: 288 us
  waiting for transfers between devices  115 us (40%)
  other arithmetic  62.1 us (21%)
  blocking collectives  50.1 us (17%)
  matrix products  23.9 us (8%)
  local copies, waits for them, and re-layouts  14.1 us (5%)
  between operations  13.8 us (5%)
  loops' own time  8.66 us (3%)
    reduce_scatter x1, waiting for transfers between devices, on_device(): lax.psum_scatter(totals[1], 'item', scatter_dimension=0, tiled=True)  33.1 us
    reduce_scatter x1, waiting for transfers between devices, on_device(): lax.psum_scatter(totals[0], 'item', scatter_dimension=0, tiled=True)  28.4 us
    reduce_scatter x1, waiting for transfers between devices, on_device(): lax.psum_scatter(totals[2], 'pb', scatter_dimension=0, tiled=True)  27.4 us
    reduce_scatter x1, waiting for transfers between devices, on_device(): lax.psum_scatter(totals[3], 'pb', scatter_dimension=0, tiled=True)  25.8 us
    reduce_sum x6, other arithmetic, tile_grads(): jnp.sum(gate_grad, axis=1)  17.5 us
    dynamic_update_slice x24, other arithmetic, accumulate(): lax.dynamic_update_slice_in_dim(total, lax.dynamic_slice_in_dim(total, st...  17.5 us
    all_gather x1, blocking collectives, on_device(): lax.all_gather(queries, 'item', axis=0, tiled=True)  15 us
    all_gather x1, blocking collectives, on_device(): lax.all_gather(gate_query, 'item', axis=0, tiled=True)  14.5 us
  transfers between devices with their start and end apart: 4, of which 4 were waited for; matrix products, arithmetic and copies ran while one was open for 2% of the time, Pallas kernels for 0%

commit v1 on v0

v1 whole, which is shorter than its diff:
```python
import functools

import jax
import jax.numpy as jnp
from jax import lax
from jax.experimental import pallas as pl
from jax.experimental.pallas import tpu as pltpu
from jax.sharding import PartitionSpec as P

E = 64
KQ = 8
KI = 8
C = KQ * KI
MESH = pl.DeviceIdType.MESH
BF = jnp.bfloat16
F32 = jnp.float32
VMEM_BYTES = 48 * 1024 * 1024


def dot_nn(x, y):
    return lax.dot_general(x, y, (((1,), (0,)), ((), ())), preferred_element_type=F32)


def dot_nt(x, y):
    return lax.dot_general(x, y, (((1,), (1,)), ((), ())), preferred_element_type=F32)


def dot_tn(x, y):
    return lax.dot_general(x, y, (((0,), (0,)), ((), ())), preferred_element_type=F32)


def eye(size):
    rows = lax.broadcasted_iota(jnp.int32, (size, size), 0)
    cols = lax.broadcasted_iota(jnp.int32, (size, size), 1)
    return jnp.where(rows == cols, 1.0, 0.0).astype(BF)


def split(x):
    high = x.astype(BF)
    return high, (x - high.astype(F32)).astype(BF)


def greet(devices):
    barrier = pltpu.get_barrier_semaphore()
    for device in devices:
        pl.semaphore_signal(barrier, inc=1, device_id=device, device_id_type=MESH)
    pl.semaphore_wait(barrier, len(devices))


def places(n_pb, n_item):
    p, j = lax.axis_index("pb"), lax.axis_index("item")
    sibling = j + 1 - 2 * lax.rem(j, 2)
    peers = [lax.rem(j + 2 * k, n_item) for k in range(1, n_item // 2)]
    rows = [lax.rem(p + k, n_pb) for k in range(1, n_pb)]
    return p, j, sibling, peers, rows


def send(src, dst, sems, device):
    copy = pltpu.make_async_remote_copy(
        src_ref=src, dst_ref=dst, send_sem=sems[0], recv_sem=sems[1],
        device_id=device, device_id_type=MESH,
    )
    copy.start()
    return copy


def gather_kernel(n_pb, n_item, q_ref, gq_ref, i_ref, gi_ref, bq, bgq, bi, bgi,
                  z_send, z_recv, f_send, f_recv, i_send, i_recv, local_sem):
    p, j, sibling, peers, rows = places(n_pb, n_item)
    greet([(p, sibling)] + [(p, peer) for peer in peers] + [(row, j) for row in rows])
    q_rows, i_rows = q_ref.shape[0], i_ref.shape[0]

    def q_at(ref, index):
        return ref.at[pl.ds(pl.multiple_of(index * q_rows, q_rows), q_rows)]

    def i_at(ref, index):
        return ref.at[pl.ds(pl.multiple_of(index * i_rows, i_rows), i_rows)]

    sides = ((q_ref, bq), (gq_ref, bgq))
    copies, arrivals = [], []
    for k, peer in enumerate(peers):
        arrivals.append([send(src, q_at(dst, j), (z_send.at[k, m], z_recv.at[k, m]), (p, peer))
                         for m, (src, dst) in enumerate(sides)])
    for k, row in enumerate(rows):
        copies += [send(src, i_at(dst, p), (i_send.at[k, m], i_recv.at[k, m]), (row, j))
                   for m, (src, dst) in enumerate(((i_ref, bi), (gi_ref, bgi)))]
    copies += [send(src, q_at(dst, j), (f_send.at[0, m], f_recv.at[0, m]), (p, sibling))
               for m, (src, dst) in enumerate(sides)]
    local = [pltpu.make_async_copy(q_ref, q_at(bq, j), local_sem.at[0]),
             pltpu.make_async_copy(gq_ref, q_at(bgq, j), local_sem.at[1]),
             pltpu.make_async_copy(i_ref, i_at(bi, p), local_sem.at[2]),
             pltpu.make_async_copy(gi_ref, i_at(bgi, p), local_sem.at[3])]
    for copy in local:
        copy.start()
    for k in range(len(peers)):
        source = lax.rem(j + n_item - 2 * (k + 1), n_item)
        for m, dst in enumerate((bq, bgq)):
            arrivals[k][m].wait_recv()
            copies.append(send(q_at(dst, source), q_at(dst, source),
                               (f_send.at[k + 1, m], f_recv.at[k + 1, m]), (p, sibling)))
    for pair in arrivals:
        for copy in pair:
            copy.wait_send()
    for copy in copies:
        copy.wait()
    for copy in local:
        copy.wait()


def gather(n_pb, n_item, queries, gate_query, items, gate_items):
    def whole(x, n):
        return jax.ShapeDtypeStruct((x.shape[0] * n, x.shape[1]), x.dtype)

    half = n_item // 2
    dma = pltpu.SemaphoreType.DMA
    return pl.pallas_call(
        functools.partial(gather_kernel, n_pb, n_item),
        out_shape=(whole(queries, n_item), whole(gate_query, n_item),
                   whole(items, n_pb), whole(gate_items, n_pb)),
        in_specs=[pl.BlockSpec(memory_space=pl.ANY)] * 4,
        out_specs=(pl.BlockSpec(memory_space=pl.ANY),) * 4,
        scratch_shapes=[dma((max(half - 1, 1), 2)), dma((max(half - 1, 1), 2)), dma((half, 2)), dma((half, 2)),
                        dma((max(n_pb - 1, 1), 2)), dma((max(n_pb - 1, 1), 2)), dma((4,))],
        compiler_params=pltpu.CompilerParams(collective_id=0, has_side_effects=True),
        name="gather_blocks",
    )(queries, gate_query, items, gate_items)


def compute_kernel(tiles, bq, bgq, bi, bgi, d_ref, dq, dgq, di, dgi,
                   qt, it, at, bt, qx, ix, s, u, v, dqt, dit, gqt, git):
    nq, width = bq.shape
    ni = bi.shape[0]
    slots, extent = d_ref.shape[0], d_ref.shape[1]
    item_blocks = ni // extent
    eye_w = eye(width)
    eye_c = eye(C)
    qt[...] = dot_nt(eye_w, bq[...])
    it[...] = dot_nt(eye_w, bi[...])

    def gate_factors(ref):
        gates = dot_nt(eye_c, ref[...])
        return jnp.exp(gates - jnp.max(gates, axis=0, keepdims=True))

    at[...] = gate_factors(bgq)
    bt[...] = gate_factors(bgi)
    s[...] = jnp.zeros_like(s)
    dit[...] = jnp.zeros_like(dit)

    def span(a):
        return pl.ds(pl.multiple_of(a * KI * E, KI * E), KI * E)

    @pl.loop(0, KQ)
    def _(a):
        part = qt[pl.ds(pl.multiple_of(a * E, E), E), :]
        a_rows = at[pl.ds(pl.multiple_of(a * KI, KI), KI), :]
        b_rows = bt[pl.ds(pl.multiple_of(a * KI, KI), KI), :]
        for b in range(KI):
            at_b = pl.ds(pl.multiple_of((a * KI + b) * E, E), E)
            qx[at_b, :] = (a_rows[b:b + 1] * part).astype(BF)
            ix[at_b, :] = (b_rows[b:b + 1] * it[b * E:(b + 1) * E, :]).astype(BF)
        s[...] += dot_tn(qx[span(a), :], ix[span(a), :])

    a_high, a_low = split(at[...])
    b_high, b_low = split(bt[...])
    total = dot_tn(jnp.concatenate([a_high, a_high, a_low], axis=0),
                   jnp.concatenate([b_high, b_low, b_high], axis=0))
    for qb in range(nq // extent):
        here = slice(qb * extent, (qb + 1) * extent)
        for ib in range(item_blocks):
            there = slice(ib * extent, (ib + 1) * extent)
            tile_id = qb * item_blocks + ib
            t = jnp.zeros((extent, extent), F32)
            for slot in range(slots):
                t = jnp.where(tiles[0, slot] == tile_id, d_ref[slot].astype(F32), t)
            scale = 1.0 / total[here, there]
            rounded = (t * scale).astype(BF)
            u[here, there] = rounded
            v[here, there] = rounded.astype(F32) * (s[here, there] * scale)

    @pl.loop(0, KQ)
    def _(a):
        item_side = dot_nn(qx[span(a), :], u[...])
        query_side = dot_nt(ix[span(a), :], u[...])
        gates = pl.ds(pl.multiple_of(a * KI, KI), KI)
        a_rows = at[gates, :]
        b_rows = bt[gates, :]
        query_sum = jnp.zeros((E, nq), F32)
        query_rows, item_rows = [], []
        for b in range(KI):
            rows = slice(b * E, (b + 1) * E)
            at_b = pl.ds(pl.multiple_of((a * KI + b) * E, E), E)
            query_sum += a_rows[b:b + 1] * query_side[rows]
            query_rows.append(jnp.sum(qx[at_b, :].astype(F32) * query_side[rows], axis=0, keepdims=True))
            dit[rows, :] += b_rows[b:b + 1] * item_side[rows]
            item_rows.append(jnp.sum(ix[at_b, :].astype(F32) * item_side[rows], axis=0, keepdims=True))
        dqt[pl.ds(pl.multiple_of(a * E, E), E), :] = query_sum.astype(BF)
        gqt[gates, :] = jnp.concatenate(query_rows, axis=0)
        git[gates, :] = jnp.concatenate(item_rows, axis=0)

    v_high, v_low = split(v[...])
    a_both = jnp.concatenate([a_high, a_low], axis=0)
    b_both = jnp.concatenate([b_high, b_low], axis=0)
    q_second = dot_nt(b_both, v_high)
    q_second = q_second[:C] + q_second[C:] + dot_nt(b_high, v_low)
    i_second = dot_nn(a_both, v_high)
    i_second = i_second[:C] + i_second[C:] + dot_nn(a_high, v_low)
    eye_q, eye_i = eye(nq), eye(ni)
    dq[...] = dot_nt(eye_q, dqt[...]).astype(BF)
    di[...] = dot_nt(eye_i, dit[...].astype(BF)).astype(BF)
    dgq[...] = dot_nt(eye_q, (gqt[...] - at[...] * q_second).astype(BF)).astype(BF)
    dgi[...] = dot_nt(eye_i, (git[...] - bt[...] * i_second).astype(BF)).astype(BF)


def compute(slot_tiles, bq, bgq, bi, bgi, d_scores):
    nq, width = bq.shape
    ni = bi.shape[0]
    vmem = pl.BlockSpec(memory_space=pltpu.VMEM)
    scratch = [((width, nq), F32), ((width, ni), F32), ((C, nq), F32), ((C, ni), F32),
               ((C * E, nq), BF), ((C * E, ni), BF), ((nq, ni), F32), ((nq, ni), BF), ((nq, ni), F32),
               ((width, nq), BF), ((width, ni), F32), ((C, nq), F32), ((C, ni), F32)]
    return pl.pallas_call(
        compute_kernel,
        out_shape=tuple(jax.ShapeDtypeStruct(x.shape, BF) for x in (bq, bgq, bi, bgi)),
        in_specs=[pl.BlockSpec(memory_space=pltpu.SMEM)] + [vmem] * 5,
        out_specs=(vmem,) * 4,
        scratch_shapes=[pltpu.VMEM(shape, kind) for shape, kind in scratch],
        compiler_params=pltpu.CompilerParams(vmem_limit_bytes=VMEM_BYTES),
        name="tile_gradients",
    )(slot_tiles, bq, bgq, bi, bgi, d_scores)


def reduce_kernel(n_pb, n_item, dq, dgq, di, dgi, oq, ogq, oi, ogi,
                  near_q, near_g, out_q, out_g, far_q, far_g, item_q, item_g,
                  f_send, f_recv, z_send, z_recv, i_send, i_recv):
    p, j, sibling, peers, rows = places(n_pb, n_item)
    greet([(p, sibling)] + [(p, peer) for peer in peers] + [(row, j) for row in rows])
    q_rows, i_rows = oq.shape[0], oi.shape[0]

    def q_at(index):
        return pl.ds(pl.multiple_of(index * q_rows, q_rows), q_rows)

    def i_at(index):
        return pl.ds(pl.multiple_of(index * i_rows, i_rows), i_rows)

    mine = [j] + peers
    theirs = [x + sibling - j for x in mine]
    order = list(range(1, len(mine))) + [0]
    near = {}
    for k in order:
        near[k] = [send(src.at[q_at(theirs[k])], dst.at[k], (f_send.at[k, m], f_recv.at[k, m]), (p, sibling))
                   for m, (src, dst) in enumerate(((dq, near_q), (dgq, near_g)))]
    item_copies = []
    for k, row in enumerate(rows):
        item_copies += [send(src.at[i_at(row)], dst.at[k], (i_send.at[k, m], i_recv.at[k, m]), (row, j))
                        for m, (src, dst) in enumerate(((di, item_q), (dgi, item_g)))]
    far = []
    for k, peer in enumerate(peers):
        for m, (src, got, staged, dst) in enumerate(((dq, near_q, out_q, far_q), (dgq, near_g, out_g, far_g))):
            near[k + 1][m].wait_recv()
            staged[k] = (src[q_at(peer), :].astype(F32) + got[k + 1].astype(F32)).astype(BF)
            far.append(send(staged.at[k], dst.at[k], (z_send.at[k, m], z_recv.at[k, m]), (p, peer)))
    for copy in near[0]:
        copy.wait_recv()
    for copy in item_copies:
        copy.wait_recv()
    for src, got, out, place in ((di, item_q, oi, i_at(p)), (dgi, item_g, ogi, i_at(p))):
        total = src[place, :].astype(F32)
        for k in range(len(rows)):
            total += got[k].astype(F32)
        out[...] = total.astype(out.dtype)
    for copy in far:
        copy.wait_recv()
    for src, got, more, out in ((dq, near_q, far_q, oq), (dgq, near_g, far_g, ogq)):
        total = src[q_at(j), :].astype(F32) + got[0].astype(F32)
        for k in range(len(peers)):
            total += more[k].astype(F32)
        out[...] = total.astype(out.dtype)
    for k in order:
        for copy in near[k]:
            copy.wait_send()
    for copy in item_copies + far:
        copy.wait_send()


def reduce(n_pb, n_item, dq, dgq, di, dgi):
    half = n_item // 2
    peers, rows = max(half - 1, 1), max(n_pb - 1, 1)
    q_rows, i_rows = dq.shape[0] // n_item, di.shape[0] // n_pb
    width = dq.shape[1]
    dma = pltpu.SemaphoreType.DMA
    vmem = pl.BlockSpec(memory_space=pltpu.VMEM)
    shapes = [(half, q_rows, width), (half, q_rows, C), (peers, q_rows, width), (peers, q_rows, C),
              (peers, q_rows, width), (peers, q_rows, C), (rows, i_rows, width), (rows, i_rows, C)]
    return pl.pallas_call(
        functools.partial(reduce_kernel, n_pb, n_item),
        out_shape=(jax.ShapeDtypeStruct((q_rows, width), BF), jax.ShapeDtypeStruct((q_rows, C), F32),
                   jax.ShapeDtypeStruct((i_rows, width), BF), jax.ShapeDtypeStruct((i_rows, C), F32)),
        in_specs=[vmem] * 4,
        out_specs=(vmem,) * 4,
        scratch_shapes=[pltpu.VMEM(shape, BF) for shape in shapes]
        + [dma((half, 2)), dma((half, 2)), dma((peers, 2)), dma((peers, 2)), dma((rows, 2)), dma((rows, 2))],
        compiler_params=pltpu.CompilerParams(collective_id=1, has_side_effects=True,
                                             vmem_limit_bytes=VMEM_BYTES),
        name="reduce_blocks",
    )(dq, dgq, di, dgi)


def on_device(n_pb, n_item, queries, gate_query, items, gate_items, slot_tiles, d_scores):
    blocks = gather(n_pb, n_item, queries, gate_query, items, gate_items)
    extent = d_scores.shape[-1]
    partial = compute(slot_tiles, *blocks, d_scores.reshape(-1, extent, extent))
    return reduce(n_pb, n_item, *partial)


def solution(mesh):
    return jax.shard_map(
        functools.partial(on_device, mesh.shape["pb"], mesh.shape["item"]),
        mesh=mesh,
        in_specs=(
            P(("pb", "item"), None),
            P(("pb", "item"), None),
            P(("item", "pb"), None),
            P(("item", "pb"), None),
            P("pb", "item"),
            P("pb", "item", None, None),
        ),
        out_specs=(
            P(("pb", "item"), None),
            P(("pb", "item"), None),
            P(("item", "pb"), None),
            P(("item", "pb"), None),
        ),
        check_vma=False,
    )
```

time: 289 us -> 51.5 us (0.18)
  waiting for transfers between devices: 115 us -> 0 us
  other arithmetic: 62.1 us -> 0 us
  blocking collectives: 50.1 us -> 0 us
  Pallas kernels: 0 us -> 41.9 us
  matrix products: 23.9 us -> 0 us
  between operations: 13.8 us -> 0.68 us
  loops' own time: 8.66 us -> 0 us
  local copies, waits for them, and re-layouts: 14.1 us -> 8.6 us
    reduce_scatter x4 -> x0, waiting for transfers between devices: 115 us -> none  [the longest x1 33.1 us: on_device(): lax.psum_scatter(totals[1], 'item', scatter_dimension=0, tiled=True)]
    all_gather x4 -> x0, blocking collectives: 50.1 us -> none  [the longest x1 15 us: on_device(): lax.all_gather(queries, 'item', axis=0, tiled=True)]
    pallas_call x0 -> x3, Pallas kernels: none -> 41.9 us  [the longest x1 15.1 us: gather(): pl.pallas_call(functools.partial(gather_kernel, n_pb, n_item), out_shape=...]
    reduce_sum x12 -> x0, other arithmetic: 25.1 us -> none  [the longest x6 17.5 us: tile_grads(): jnp.sum(gate_grad, axis=1)]
    dot_general x18 -> x0, matrix products: 23.9 us -> none  [the longest x6 8.07 us: tile_grads(): jnp.einsum('abqi,qae->ibe', logit_parts, query_parts, preferred_element_t...]
    dynamic_update_slice x24 -> x0, other arithmetic: 17.5 us -> none  [accumulate(): lax.dynamic_update_slice_in_dim(total, lax.dynamic_slice_in_dim(total, st...]
    another operation x7 -> x0, loops' own time: 8.66 us -> none  [the longest x6 4.72 us: home_step(): return lax.cond(tile_id >= 0, work, lambda state: state, current)]
    reduce_max x6 -> x0, other arithmetic: 7.42 us -> none  [tile_grads(): weights = jax.nn.softmax(gates, axis=0)]
  transfers between devices with their start and end apart: 4 -> 0, of which waited for: 4 -> 0; matrix products, arithmetic and copies ran while one was open for 2% -> 0% of each run, Pallas kernels for 0% -> 0%
where the time goes in v1:
time: 51.5 us; the launch traced here: 51.2 us
  Pallas kernels  41.9 us (81%)
  local copies, waits for them, and re-layouts  8.6 us (17%)
  between operations  0.68 us (1%)
    pallas_call x1, Pallas kernels, gather(): pl.pallas_call(functools.partial(gather_kernel, n_pb, n_item), out_shape=...  15.1 us
    pallas_call x1, Pallas kernels, compute(): pl.pallas_call(compute_kernel, out_shape=tuple((jax.ShapeDtypeStruct(x.sh...  14.5 us
    pallas_call x1, Pallas kernels, reduce(): pl.pallas_call(functools.partial(reduce_kernel, n_pb, n_item), out_shape=...  12.4 us
    unnamed x16, local copies, waits for them, and re-layouts  7.91 us

profile of v1, /device:TPU:0, one launch (start us, length us, event | category | flops | bytes accessed | tf_op | source)
XLA Modules:
  0.0 51.2 jit_solution(15035476833854530191)
XLA Ops:
  0.6 0.0 copy-start.2
  0.6 1.5 %copy.10.gi_ref = bf16[128,64]{1,0:T(8,128)(2,1)} copy(bf16[128,64]{0,1:T(8,128)(2,1)} %param.9) | data formatting | bytes 32768 | tf_op args[3]
  2.1 15.1 %gather_blocks.1 = (bf16[512,512]{1,0:T(8,128)(2,1)}, bf16[512,64]{1,0:T(8,128)(2,1)}, bf16[512,512]{1,0:T(8,128)(2,1)}, bf16[512,64]{1,0:T(8,128)(2,1)}) custom-call(bf16[64,512]{1,0:T(8,128)(2,1)} %q_ref.1, bf16[64,64]{1,0:T(8,128)(2,1)} %gq_ref.1, bf16[128,512]{1,0:T(8,128)(2,1)} %i_ref.1, bf16[128,64]{1,0:T(8,128)(2,1)} %copy.10.gi_ref), custom_call_target="tpu_custom_call" | custom-call | tf_op jit(solution)/shard_map/gather_blocks/pallas_call | solution.py:116
  17.2 0.0 copy-start.5
  17.2 0.0 copy-done.2
  17.2 0.6 %copy-done.5 = s32[1,6]{1,0:T(1,128)S(1)} copy-done((s32[1,6]{1,0:T(1,128)S(1)}, s32[1,6]{1,0:T(1,128)}, u32[]{:S(2)}) %copy-start.5) | copy-done | bytes 48
  17.9 0.0 copy-start
  17.9 1.0 %copy-done = bf16[512,512]{1,0:T(8,128)(2,1)S(1)} copy-done((bf16[512,512]{1,0:T(8,128)(2,1)S(1)}, bf16[512,512]{1,0:T(8,128)(2,1)}, u32[]{:S(2)}) %copy-start) | copy-done | bytes 524312
  18.9 0.0 copy-start.1
  18.9 1.0 %copy-done.1 = bf16[512,512]{1,0:T(8,128)(2,1)S(1)} copy-done((bf16[512,512]{1,0:T(8,128)(2,1)S(1)}, bf16[512,512]{1,0:T(8,128)(2,1)}, u32[]{:S(2)}) %copy-start.1) | copy-done | bytes 524312
  19.9 0.0 copy-start.3
  19.9 0.9 %copy-done.3 = bf16[512,64]{1,0:T(8,128)(2,1)S(1)} copy-done((bf16[512,64]{1,0:T(8,128)(2,1)S(1)}, bf16[512,64]{1,0:T(8,128)(2,1)}, u32[]{:S(2)}) %copy-start.3) | copy-done | bytes 65560
  20.8 0.0 copy-start.4
  20.8 0.9 %copy-done.4 = bf16[512,64]{1,0:T(8,128)(2,1)S(1)} copy-done((bf16[512,64]{1,0:T(8,128)(2,1)S(1)}, bf16[512,64]{1,0:T(8,128)(2,1)}, u32[]{:S(2)}) %copy-start.4) | copy-done | bytes 65560
  21.7 14.5 %tile_gradients.1 = (bf16[512,512]{1,0:T(8,128)(2,1)S(1)}, bf16[512,64]{1,0:T(8,128)(2,1)S(1)}, bf16[512,512]{1,0:T(8,128)(2,1)S(1)}, bf16[512,64]{1,0:T(8,128)(2,1)S(1)}) custom-call(s32[1,6]{1,0:T(1,128)S(1)} %copy-done.5, bf16[512,512]{1,0:T(8,128)(2,1)S(1)} %copy-done, bf16[512,64]{1,0:T(8,128)(2,1)S(1)} %copy-done.3, bf16[512,512]{1,0:T(8,128)(2,1)S(1)} %copy-done.1, ...), custom_call_target="tpu_custom_call" | custom-call | tf_op jit(solution)/shard_map/tile_gradients/pallas_call | solution.py:221
  36.2 12.4 %reduce_blocks.1 = (bf16[64,512]{1,0:T(8,128)(2,1)S(1)}, f32[64,64]{1,0:T(8,128)S(1)}, bf16[128,512]{1,0:T(8,128)(2,1)S(1)}, f32[128,64]{1,0:T(8,128)S(1)}) custom-call(bf16[512,512]{1,0:T(8,128)(2,1)S(1)} %get-tuple-element.16.dq, bf16[512,64]{1,0:T(8,128)(2,1)S(1)} %get-tuple-element.17.dgq, bf16[512,512]{1,0:T(8,128)(2,1)S(1)} %get-tuple-element.18.di, ...), custom_call_target="tpu_custom_call" | custom-call | tf_op jit(solution)/shard_map/reduce_blocks/pallas_call | solution.py:294
  48.6 0.7 %copy.11 = f32[128,64]{0,1:T(8,128)} copy(f32[128,64]{1,0:T(8,128)S(1)} %get-tuple-element.23) | data formatting | bytes 65536 | tf_op jit(solution)/shard_map/reduce_blocks/pallas_call | solution.py:294
  49.3 0.6 %copy.15 = bf16[64,512]{1,0:T(8,128)(2,1)} copy(bf16[64,512]{1,0:T(8,128)(2,1)S(1)} %get-tuple-element.28) | data formatting | bytes 131072
  50.0 0.6 %copy.16 = f32[64,64]{1,0:T(8,128)} copy(f32[64,64]{1,0:T(8,128)S(1)} %get-tuple-element.29) | data formatting | bytes 32768
  50.6 0.7 %copy.17 = bf16[128,512]{1,0:T(8,128)(2,1)} copy(bf16[128,512]{1,0:T(8,128)(2,1)S(1)} %get-tuple-element.30) | data formatting | bytes 262144
Async XLA Ops:
  0.6 16.6 %copy-start.2 = (bf16[1,6,128,128]{3,2,1,0:T(8,128)(2,1)S(1)}, bf16[1,6,128,128]{3,2,1,0:T(8,128)(2,1)}, u32[]{:S(2)}) copy-start(bf16[1,6,128,128]{3,2,1,0:T(8,128)(2,1)} %param.11) | copy-start | bytes 589828
  17.2 0.7 %copy-start.5 = (s32[1,6]{1,0:T(1,128)S(1)}, s32[1,6]{1,0:T(1,128)}, u32[]{:S(2)}) copy-start(s32[1,6]{1,0:T(1,128)} %tiles.1) | copy-start | bytes 76
  17.9 1.0 %copy-start = (bf16[512,512]{1,0:T(8,128)(2,1)S(1)}, bf16[512,512]{1,0:T(8,128)(2,1)}, u32[]{:S(2)}) copy-start(bf16[512,512]{1,0:T(8,128)(2,1)} %get-tuple-element.12.bq) | copy-start | bytes 1572868
  18.9 1.0 %copy-start.1 = (bf16[512,512]{1,0:T(8,128)(2,1)S(1)}, bf16[512,512]{1,0:T(8,128)(2,1)}, u32[]{:S(2)}) copy-start(bf16[512,512]{1,0:T(8,128)(2,1)} %get-tuple-element.14.bi) | copy-start | bytes 1572868
  19.9 0.9 %copy-start.3 = (bf16[512,64]{1,0:T(8,128)(2,1)S(1)}, bf16[512,64]{1,0:T(8,128)(2,1)}, u32[]{:S(2)}) copy-start(bf16[512,64]{1,0:T(8,128)(2,1)} %get-tuple-element.13.bgq) | copy-start | bytes 196612
  20.8 0.9 %copy-start.4 = (bf16[512,64]{1,0:T(8,128)(2,1)S(1)}, bf16[512,64]{1,0:T(8,128)(2,1)}, u32[]{:S(2)}) copy-start(bf16[512,64]{1,0:T(8,128)(2,1)} %get-tuple-element.15.bgi) | copy-start | bytes 196612

commit v2 on v1

v2 whole, which is shorter than its diff:
```python
import functools

import jax
import jax.numpy as jnp
from jax import lax
from jax.experimental import pallas as pl
from jax.experimental.pallas import tpu as pltpu
from jax.sharding import PartitionSpec as P

E = 64
KQ = 8
KI = 8
C = KQ * KI
MESH = pl.DeviceIdType.MESH
BF = jnp.bfloat16
F32 = jnp.float32
VMEM_BYTES = 48 * 1024 * 1024


def dot_nn(x, y):
    return lax.dot_general(x, y, (((1,), (0,)), ((), ())), preferred_element_type=F32)


def dot_nt(x, y):
    return lax.dot_general(x, y, (((1,), (1,)), ((), ())), preferred_element_type=F32)


def dot_tn(x, y):
    return lax.dot_general(x, y, (((0,), (0,)), ((), ())), preferred_element_type=F32)


def eye(size):
    rows = lax.broadcasted_iota(jnp.int32, (size, size), 0)
    cols = lax.broadcasted_iota(jnp.int32, (size, size), 1)
    return jnp.where(rows == cols, 1.0, 0.0).astype(BF)


def split(x):
    high = x.astype(BF)
    return high, (x - high.astype(F32)).astype(BF)


def greet(devices):
    barrier = pltpu.get_barrier_semaphore()
    for device in devices:
        pl.semaphore_signal(barrier, inc=1, device_id=device, device_id_type=MESH)
    pl.semaphore_wait(barrier, len(devices))


def places(n_pb, n_item):
    p, j = lax.axis_index("pb"), lax.axis_index("item")
    sibling = j + 1 - 2 * lax.rem(j, 2)
    peers = [lax.rem(j + 2 * k, n_item) for k in range(1, n_item // 2)]
    rows = [lax.rem(p + k, n_pb) for k in range(1, n_pb)]
    return p, j, sibling, peers, rows


def send(src, dst, sems, device):
    copy = pltpu.make_async_remote_copy(
        src_ref=src, dst_ref=dst, send_sem=sems[0], recv_sem=sems[1],
        device_id=device, device_id_type=MESH,
    )
    copy.start()
    return copy


def kernel(n_pb, n_item, tiles, q_ref, gq_ref, i_ref, gi_ref, d_hbm, oq, ogq, oi, ogi,
           bq, bgq, bi, bgi, d_ref, qt, it, at, bt, qx, ix, s, u, v, dqt, dit, gqt, git,
           dq, dgq, di, dgi, near_q, near_g, out_q, out_g, far_q, far_g, item_q, item_g,
           z_send, z_recv, f_send, f_recv, i_send, i_recv,
           rz_send, rz_recv, rf_send, rf_recv, ri_send, ri_recv, local_sem):
    p, j, sibling, peers, others = places(n_pb, n_item)
    greet([(p, sibling)] + [(p, peer) for peer in peers] + [(row, j) for row in others])
    q_rows, i_rows = q_ref.shape[0], i_ref.shape[0]
    nq, width = bq.shape
    ni = bi.shape[0]
    slots, extent = d_ref.shape[0], d_ref.shape[1]
    item_blocks = ni // extent

    def q_at(index):
        return pl.ds(pl.multiple_of(index * q_rows, q_rows), q_rows)

    def i_at(index):
        return pl.ds(pl.multiple_of(index * i_rows, i_rows), i_rows)

    sides = ((q_ref, bq), (gq_ref, bgq))
    copies, arrivals, item_arrivals = [], [], []
    for k, peer in enumerate(peers):
        arrivals.append([send(src, dst.at[q_at(j)], (z_send.at[k, m], z_recv.at[k, m]), (p, peer))
                         for m, (src, dst) in enumerate(sides)])
    for k, row in enumerate(others):
        item_arrivals += [send(i_ref, bi.at[i_at(p)], (i_send.at[k, 0], i_recv.at[k, 0]), (row, j)),
                          send(gi_ref, bgi.at[p], (i_send.at[k, 1], i_recv.at[k, 1]), (row, j))]
    copies += [send(src, dst.at[q_at(j)], (f_send.at[0, m], f_recv.at[0, m]), (p, sibling))
               for m, (src, dst) in enumerate(sides)]
    local = [pltpu.make_async_copy(q_ref, bq.at[q_at(j)], local_sem.at[0]),
             pltpu.make_async_copy(gq_ref, bgq.at[q_at(j)], local_sem.at[1]),
             pltpu.make_async_copy(i_ref, bi.at[i_at(p)], local_sem.at[2]),
             pltpu.make_async_copy(gi_ref, bgi.at[p], local_sem.at[3]),
             pltpu.make_async_copy(d_hbm, d_ref, local_sem.at[4])]
    for copy in local:
        copy.start()
    s[...] = jnp.zeros_like(s)
    dit[...] = jnp.zeros_like(dit)
    for k in range(len(peers)):
        source = lax.rem(j + n_item - 2 * (k + 1), n_item)
        for m, dst in enumerate((bq, bgq)):
            arrivals[k][m].wait_recv()
            copies.append(send(dst.at[q_at(source)], dst.at[q_at(source)],
                               (f_send.at[k + 1, m], f_recv.at[k + 1, m]), (p, sibling)))
    for copy in local:
        copy.wait()
    for copy in item_arrivals:
        copy.wait_recv()

    eye_w = eye(width)

    def factors(gates):
        return jnp.exp(gates - jnp.max(gates, axis=0, keepdims=True))

    it[...] = dot_nt(eye_w, bi[...])
    bt[...] = factors(jnp.concatenate([bgi[k].astype(F32) for k in range(n_pb)], axis=1))
    for copy in copies:
        copy.wait_recv()
    qt[...] = dot_nt(eye_w, bq[...])
    at[...] = factors(dot_nt(eye(C), bgq[...]))

    def span(a):
        return pl.ds(pl.multiple_of(a * KI * E, KI * E), KI * E)

    @pl.loop(0, KQ)
    def _(a):
        part = qt[pl.ds(pl.multiple_of(a * E, E), E), :]
        a_rows = at[pl.ds(pl.multiple_of(a * KI, KI), KI), :]
        b_rows = bt[pl.ds(pl.multiple_of(a * KI, KI), KI), :]
        for b in range(KI):
            at_b = pl.ds(pl.multiple_of((a * KI + b) * E, E), E)
            qx[at_b, :] = (a_rows[b:b + 1] * part).astype(BF)
            ix[at_b, :] = (b_rows[b:b + 1] * it[b * E:(b + 1) * E, :]).astype(BF)
        s[...] += dot_tn(qx[span(a), :], ix[span(a), :])

    a_high, a_low = split(at[...])
    b_high, b_low = split(bt[...])
    total = dot_tn(jnp.concatenate([a_high, a_high, a_low], axis=0),
                   jnp.concatenate([b_high, b_low, b_high], axis=0))
    for qb in range(nq // extent):
        here = slice(qb * extent, (qb + 1) * extent)
        for ib in range(item_blocks):
            there = slice(ib * extent, (ib + 1) * extent)
            tile_id = qb * item_blocks + ib
            t = jnp.zeros((extent, extent), F32)
            for slot in range(slots):
                t = jnp.where(tiles[0, slot] == tile_id, d_ref[slot].astype(F32), t)
            scale = 1.0 / total[here, there]
            rounded = (t * scale).astype(BF)
            u[here, there] = rounded
            v[here, there] = rounded.astype(F32) * (s[here, there] * scale)

    @pl.loop(0, KQ)
    def _(a):
        query_side = dot_nt(ix[span(a), :], u[...])
        gates = pl.ds(pl.multiple_of(a * KI, KI), KI)
        a_rows = at[gates, :]
        query_sum = jnp.zeros((E, nq), F32)
        query_rows = []
        for b in range(KI):
            rows = slice(b * E, (b + 1) * E)
            at_b = pl.ds(pl.multiple_of((a * KI + b) * E, E), E)
            query_sum += a_rows[b:b + 1] * query_side[rows]
            query_rows.append(jnp.sum(qx[at_b, :].astype(F32) * query_side[rows], axis=0, keepdims=True))
        dqt[pl.ds(pl.multiple_of(a * E, E), E), :] = query_sum.astype(BF)
        gqt[gates, :] = jnp.concatenate(query_rows, axis=0)

    v_high, v_low = split(v[...])
    q_second = dot_nt(jnp.concatenate([b_high, b_low], axis=0), v_high)
    q_second = q_second[:C] + q_second[C:] + dot_nt(b_high, v_low)
    eye_q, eye_i = eye(nq), eye(ni)
    dq[...] = dot_nt(eye_q, dqt[...]).astype(BF)
    dgq[...] = dot_nt(eye_q, (gqt[...] - at[...] * q_second).astype(BF)).astype(BF)

    mine = [j] + peers
    theirs = [x + sibling - j for x in mine]
    order = list(range(1, len(mine))) + [0]
    near = {}
    for k in order:
        near[k] = [send(src.at[q_at(theirs[k])], dst.at[k], (rf_send.at[k, m], rf_recv.at[k, m]), (p, sibling))
                   for m, (src, dst) in enumerate(((dq, near_q), (dgq, near_g)))]

    def item_step(a):
        item_side = dot_nn(qx[span(a), :], u[...])
        gates = pl.ds(pl.multiple_of(a * KI, KI), KI)
        b_rows = bt[gates, :]
        item_rows = []
        for b in range(KI):
            rows = slice(b * E, (b + 1) * E)
            at_b = pl.ds(pl.multiple_of((a * KI + b) * E, E), E)
            dit[rows, :] += b_rows[b:b + 1] * item_side[rows]
            item_rows.append(jnp.sum(ix[at_b, :].astype(F32) * item_side[rows], axis=0, keepdims=True))
        git[gates, :] = jnp.concatenate(item_rows, axis=0)

    pl.loop(0, KQ // 4)(item_step)
    far = []
    for k, peer in enumerate(peers):
        for m, (src, got, staged, dst) in enumerate(((dq, near_q, out_q, far_q), (dgq, near_g, out_g, far_g))):
            near[k + 1][m].wait_recv()
            staged[k] = (src[q_at(peer), :].astype(F32) + got[k + 1].astype(F32)).astype(BF)
            far.append(send(staged.at[k], dst.at[k], (rz_send.at[k, m], rz_recv.at[k, m]), (p, peer)))
    pl.loop(KQ // 4, KQ)(item_step)

    di[...] = dot_nt(eye_i, dit[...].astype(BF)).astype(BF)
    item_copies = [send(di.at[i_at(row)], item_q.at[k], (ri_send.at[k, 0], ri_recv.at[k, 0]), (row, j))
                   for k, row in enumerate(others)]
    i_second = dot_nn(jnp.concatenate([a_high, a_low], axis=0), v_high)
    i_second = i_second[:C] + i_second[C:] + dot_nn(a_high, v_low)
    gate_sum = (git[...] - bt[...] * i_second).astype(BF)
    for k in range(n_pb):
        dgi[k] = gate_sum[:, k * i_rows:(k + 1) * i_rows]
    item_copies += [send(dgi.at[row], item_g.at[k], (ri_send.at[k, 1], ri_recv.at[k, 1]), (row, j))
                    for k, row in enumerate(others)]

    for copy in near[0] + far:
        copy.wait_recv()
    for src, got, more, out in ((dq, near_q, far_q, oq), (dgq, near_g, far_g, ogq)):
        total = src[q_at(j), :].astype(F32) + got[0].astype(F32)
        for k in range(len(peers)):
            total += more[k].astype(F32)
        out[...] = total.astype(out.dtype)
    for copy in item_copies:
        copy.wait_recv()
    for own, got, out in ((di[i_at(p), :], item_q, oi), (dgi[p], item_g, ogi)):
        total = own.astype(F32)
        for k in range(len(others)):
            total += got[k].astype(F32)
        out[...] = total.astype(out.dtype)
    for pair in arrivals + [near[k] for k in order]:
        for copy in pair:
            copy.wait_send()
    for copy in copies + item_arrivals + item_copies + far:
        copy.wait_send()


def on_device(n_pb, n_item, queries, gate_query, items, gate_items, slot_tiles, d_scores):
    extent = d_scores.shape[-1]
    cotangents = d_scores.reshape(-1, extent, extent)
    q_rows, width = queries.shape
    i_rows = items.shape[0]
    nq, ni = q_rows * n_item, i_rows * n_pb
    half = n_item // 2
    peers, others = max(half - 1, 1), max(n_pb - 1, 1)
    vmem = pl.BlockSpec(memory_space=pltpu.VMEM)
    hbm = pl.BlockSpec(memory_space=pl.ANY)
    scratch = [((nq, width), BF), ((nq, C), BF), ((ni, width), BF), ((n_pb, C, i_rows), BF), (cotangents.shape, BF),
               ((width, nq), F32), ((width, ni), F32), ((C, nq), F32), ((C, ni), F32),
               ((C * E, nq), BF), ((C * E, ni), BF), ((nq, ni), F32), ((nq, ni), BF), ((nq, ni), F32),
               ((width, nq), BF), ((width, ni), F32), ((C, nq), F32), ((C, ni), F32),
               ((nq, width), BF), ((nq, C), BF), ((ni, width), BF), ((n_pb, C, i_rows), BF),
               ((half, q_rows, width), BF), ((half, q_rows, C), BF), ((peers, q_rows, width), BF), ((peers, q_rows, C), BF),
               ((peers, q_rows, width), BF), ((peers, q_rows, C), BF), ((others, i_rows, width), BF), ((others, C, i_rows), BF)]
    sems = [(peers, 2), (peers, 2), (half, 2), (half, 2), (others, 2), (others, 2)] * 2 + [(5,)]
    out = pl.pallas_call(
        functools.partial(kernel, n_pb, n_item),
        out_shape=(jax.ShapeDtypeStruct((q_rows, width), BF), jax.ShapeDtypeStruct((q_rows, C), F32),
                   jax.ShapeDtypeStruct((i_rows, width), BF), jax.ShapeDtypeStruct((C, i_rows), F32)),
        in_specs=[pl.BlockSpec(memory_space=pltpu.SMEM)] + [hbm] * 5,
        out_specs=(vmem,) * 4,
        scratch_shapes=[pltpu.VMEM(shape, kind) for shape, kind in scratch]
        + [pltpu.SemaphoreType.DMA(shape) for shape in sems],
        compiler_params=pltpu.CompilerParams(collective_id=0, has_side_effects=True, vmem_limit_bytes=VMEM_BYTES),
        name="scoring_backward",
    )(slot_tiles, queries, gate_query, items, gate_items.T, cotangents)
    return out[0], out[1], out[2], out[3].T


def solution(mesh):
    return jax.shard_map(
        functools.partial(on_device, mesh.shape["pb"], mesh.shape["item"]),
        mesh=mesh,
        in_specs=(
            P(("pb", "item"), None),
            P(("pb", "item"), None),
            P(("item", "pb"), None),
            P(("item", "pb"), None),
            P("pb", "item"),
            P("pb", "item", None, None),
        ),
        out_specs=(
            P(("pb", "item"), None),
            P(("pb", "item"), None),
            P(("item", "pb"), None),
            P(("item", "pb"), None),
        ),
        check_vma=False,
    )
```

time: 51.5 us -> 48.1 us (0.934)
  Pallas kernels: 41.9 us -> 39.9 us
  local copies, waits for them, and re-layouts: 8.6 us -> 7.27 us
    pallas_call x3 -> x1, Pallas kernels: 41.9 us -> 39.9 us  [on_device(): pl.pallas_call(functools.partial(kernel, n_pb, n_item), out_shape=(jax.Sh...]
    pallas_call x1 -> x0, local copies, waits for them, and re-layouts: 0.7 us -> none  [reduce(): pl.pallas_call(functools.partial(reduce_kernel, n_pb, n_item), out_shape=...]
    unnamed x16, local copies, waits for them, and re-layouts: 7.91 us -> 7.27 us
where the time goes in v2:
time: 48.1 us; the launch traced here: 47.8 us
  Pallas kernels  39.9 us (83%)
  local copies, waits for them, and re-layouts  7.27 us (15%)
  between operations  0.66 us (1%)
    pallas_call x1, Pallas kernels, on_device(): pl.pallas_call(functools.partial(kernel, n_pb, n_item), out_shape=(jax.Sh...  39.9 us
    unnamed x16, local copies, waits for them, and re-layouts  7.27 us

profile of v2, /device:TPU:0, one launch (start us, length us, event | category | flops | bytes accessed | tf_op | source)
XLA Modules:
  0.0 47.8 jit_solution(14431355737458396311)
XLA Ops:
  0.6 0.0 copy-start.5
  0.6 0.6 %copy-done.5 = s32[1,6]{1,0:T(1,128)S(1)} copy-done((s32[1,6]{1,0:T(1,128)S(1)}, s32[1,6]{1,0:T(1,128)}, u32[]{:S(2)}) %copy-start.5) | copy-done | bytes 48
  1.3 0.0 copy-start
  1.3 0.9 %copy-done = bf16[1,6,128,128]{3,2,1,0:T(8,128)(2,1)S(1)} copy-done((bf16[1,6,128,128]{3,2,1,0:T(8,128)(2,1)S(1)}, bf16[1,6,128,128]{3,2,1,0:T(8,128)(2,1)}, u32[]{:S(2)}) %copy-start) | copy-done | bytes 196632
  2.2 0.0 copy-start.1
  2.2 0.9 %copy-done.1 = bf16[128,512]{1,0:T(8,128)(2,1)S(1)} copy-done((bf16[128,512]{1,0:T(8,128)(2,1)S(1)}, bf16[128,512]{1,0:T(8,128)(2,1)}, u32[]{:S(2)}) %copy-start.1) | copy-done | bytes 131096
  3.1 0.0 copy-start.2
  3.1 0.8 %copy-done.2 = bf16[64,512]{1,0:T(8,128)(2,1)S(1)} copy-done((bf16[64,512]{1,0:T(8,128)(2,1)S(1)}, bf16[64,512]{1,0:T(8,128)(2,1)}, u32[]{:S(2)}) %copy-start.2) | copy-done | bytes 65560
  4.0 0.0 copy-start.3
  4.0 0.7 %copy-done.3 = bf16[64,64]{1,0:T(8,128)(2,1)S(1)} copy-done((bf16[64,64]{1,0:T(8,128)(2,1)S(1)}, bf16[64,64]{1,0:T(8,128)(2,1)}, u32[]{:S(2)}) %copy-start.3) | copy-done | bytes 8216
  4.7 0.0 copy-start.4
  4.7 0.7 %copy-done.4 = bf16[128,64]{0,1:T(8,128)(2,1)S(1)} copy-done((bf16[128,64]{0,1:T(8,128)(2,1)S(1)}, bf16[128,64]{0,1:T(8,128)(2,1)}, u32[]{:S(2)}) %copy-start.4) | copy-done | bytes 16408
  5.4 39.9 %scoring_backward.1 = (bf16[64,512]{1,0:T(8,128)(2,1)S(1)}, f32[64,64]{1,0:T(8,128)S(1)}, bf16[128,512]{1,0:T(8,128)(2,1)S(1)}, f32[64,128]{1,0:T(8,128)S(1)}) custom-call(s32[1,6]{1,0:T(1,128)S(1)} %copy-done.5, bf16[64,512]{1,0:T(8,128)(2,1)S(1)} %copy-done.2, bf16[64,64]{1,0:T(8,128)(2,1)S(1)} %copy-done.3, bf16[128,512]{1,0:T(8,128)(2,1)S(1)} %copy-done.1, ...), custom_call_target="tpu_custom_call" | custom-call | tf_op jit(solution)/shard_map/scoring_backward/pallas_call | solution.py:260
  45.3 0.6 %copy.14 = bf16[64,512]{1,0:T(8,128)(2,1)} copy(bf16[64,512]{1,0:T(8,128)(2,1)S(1)} %get-tuple-element.16) | data formatting | bytes 131072
  45.9 0.6 %copy.15 = f32[64,64]{1,0:T(8,128)} copy(f32[64,64]{1,0:T(8,128)S(1)} %get-tuple-element.17) | data formatting | bytes 32768
  46.5 0.7 %copy.16 = bf16[128,512]{1,0:T(8,128)(2,1)} copy(bf16[128,512]{1,0:T(8,128)(2,1)S(1)} %get-tuple-element.18) | data formatting | bytes 262144
  47.2 0.6 %copy.17 = f32[128,64]{0,1:T(8,128)} copy(f32[128,64]{0,1:T(8,128)S(1)} %bitcast.4) | data formatting | bytes 65536
Async XLA Ops:
  0.6 0.7 %copy-start.5 = (s32[1,6]{1,0:T(1,128)S(1)}, s32[1,6]{1,0:T(1,128)}, u32[]{:S(2)}) copy-start(s32[1,6]{1,0:T(1,128)} %tiles.1) | copy-start | bytes 76
  1.3 0.9 %copy-start = (bf16[1,6,128,128]{3,2,1,0:T(8,128)(2,1)S(1)}, bf16[1,6,128,128]{3,2,1,0:T(8,128)(2,1)}, u32[]{:S(2)}) copy-start(bf16[1,6,128,128]{3,2,1,0:T(8,128)(2,1)} %param.11) | copy-start | bytes 589828
  2.2 0.9 %copy-start.1 = (bf16[128,512]{1,0:T(8,128)(2,1)S(1)}, bf16[128,512]{1,0:T(8,128)(2,1)}, u32[]{:S(2)}) copy-start(bf16[128,512]{1,0:T(8,128)(2,1)} %i_ref.1) | copy-start | bytes 393220
  3.1 0.8 %copy-start.2 = (bf16[64,512]{1,0:T(8,128)(2,1)S(1)}, bf16[64,512]{1,0:T(8,128)(2,1)}, u32[]{:S(2)}) copy-start(bf16[64,512]{1,0:T(8,128)(2,1)} %q_ref.1) | copy-start | bytes 196612
  4.0 0.7 %copy-start.3 = (bf16[64,64]{1,0:T(8,128)(2,1)S(1)}, bf16[64,64]{1,0:T(8,128)(2,1)}, u32[]{:S(2)}) copy-start(bf16[64,64]{1,0:T(8,128)(2,1)} %gq_ref.1) | copy-start | bytes 24580
  4.7 0.7 %copy-start.4 = (bf16[128,64]{0,1:T(8,128)(2,1)S(1)}, bf16[128,64]{0,1:T(8,128)(2,1)}, u32[]{:S(2)}) copy-start(bf16[128,64]{0,1:T(8,128)(2,1)} %param.9) | copy-start | bytes 49156

commit v3 on v2

--- a/solution.py
+++ b/solution.py
@@ -14,7 +14,7 @@
 MESH = pl.DeviceIdType.MESH
 BF = jnp.bfloat16
 F32 = jnp.float32
-VMEM_BYTES = 48 * 1024 * 1024
+VMEM_BYTES = 64 * 1024 * 1024
 
 
 def dot_nn(x, y):
@@ -51,7 +51,10 @@
     p, j = lax.axis_index("pb"), lax.axis_index("item")
     sibling = j + 1 - 2 * lax.rem(j, 2)
     peers = [lax.rem(j + 2 * k, n_item) for k in range(1, n_item // 2)]
-    rows = [lax.rem(p + k, n_pb) for k in range(1, n_pb)]
+    half = n_pb // 2
+    side, place = p // half, lax.rem(p, half)
+    rows = [(1 - side) * half + lax.rem(place + k, half) for k in range(half)]
+    rows += [side * half + lax.rem(place + k, half) for k in range(1, half)]
     return p, j, sibling, peers, rows
 
 
@@ -120,6 +123,14 @@
 
     it[...] = dot_nt(eye_w, bi[...])
     bt[...] = factors(jnp.concatenate([bgi[k].astype(F32) for k in range(n_pb)], axis=1))
+
+    @pl.loop(0, KQ)
+    def _(a):
+        b_rows = bt[pl.ds(pl.multiple_of(a * KI, KI), KI), :]
+        for b in range(KI):
+            at_b = pl.ds(pl.multiple_of((a * KI + b) * E, E), E)
+            ix[at_b, :] = (b_rows[b:b + 1] * it[b * E:(b + 1) * E, :]).astype(BF)
+
     for copy in copies:
         copy.wait_recv()
     qt[...] = dot_nt(eye_w, bq[...])
@@ -132,11 +143,9 @@
     def _(a):
         part = qt[pl.ds(pl.multiple_of(a * E, E), E), :]
         a_rows = at[pl.ds(pl.multiple_of(a * KI, KI), KI), :]
-        b_rows = bt[pl.ds(pl.multiple_of(a * KI, KI), KI), :]
         for b in range(KI):
             at_b = pl.ds(pl.multiple_of((a * KI + b) * E, E), E)
             qx[at_b, :] = (a_rows[b:b + 1] * part).astype(BF)
-            ix[at_b, :] = (b_rows[b:b + 1] * it[b * E:(b + 1) * E, :]).astype(BF)
         s[...] += dot_tn(qx[span(a), :], ix[span(a), :])
 
     a_high, a_low = split(at[...])
@@ -174,7 +183,7 @@
     v_high, v_low = split(v[...])
     q_second = dot_nt(jnp.concatenate([b_high, b_low], axis=0), v_high)
     q_second = q_second[:C] + q_second[C:] + dot_nt(b_high, v_low)
-    eye_q, eye_i = eye(nq), eye(ni)
+    eye_q, eye_i = eye(nq), eye(ni // 2)
     dq[...] = dot_nt(eye_q, dqt[...]).astype(BF)
     dgq[...] = dot_nt(eye_q, (gqt[...] - at[...] * q_second).astype(BF)).astype(BF)
 
@@ -186,37 +195,48 @@
         near[k] = [send(src.at[q_at(theirs[k])], dst.at[k], (rf_send.at[k, m], rf_recv.at[k, m]), (p, sibling))
                    for m, (src, dst) in enumerate(((dq, near_q), (dgq, near_g)))]
 
-    def item_step(a):
-        item_side = dot_nn(qx[span(a), :], u[...])
-        gates = pl.ds(pl.multiple_of(a * KI, KI), KI)
-        b_rows = bt[gates, :]
-        item_rows = []
-        for b in range(KI):
-            rows = slice(b * E, (b + 1) * E)
-            at_b = pl.ds(pl.multiple_of((a * KI + b) * E, E), E)
-            dit[rows, :] += b_rows[b:b + 1] * item_side[rows]
-            item_rows.append(jnp.sum(ix[at_b, :].astype(F32) * item_side[rows], axis=0, keepdims=True))
-        git[gates, :] = jnp.concatenate(item_rows, axis=0)
-
-    pl.loop(0, KQ // 4)(item_step)
+    def item_half(part):
+        cols = pl.ds(pl.multiple_of(part * (ni // 2), ni // 2), ni // 2)
+
+        @pl.loop(0, KQ)
+        def _(a):
+            item_side = dot_nn(qx[span(a), :], u[:, cols])
+            gates = pl.ds(pl.multiple_of(a * KI, KI), KI)
+            b_rows = bt[gates, cols]
+            item_rows = []
+            for b in range(KI):
+                rows = slice(b * E, (b + 1) * E)
+                at_b = pl.ds(pl.multiple_of((a * KI + b) * E, E), E)
+                dit[rows, cols] += b_rows[b:b + 1] * item_side[rows]
+                item_rows.append(jnp.sum(ix[at_b, cols].astype(F32) * item_side[rows], axis=0, keepdims=True))
+            git[gates, cols] = jnp.concatenate(item_rows, axis=0)
+
+        di[cols, :] = dot_nt(eye_i, dit[:, cols].astype(BF)).astype(BF)
+        high, low = split(v[:, cols])
+        second = dot_nn(jnp.concatenate([a_high, a_low], axis=0), high)
+        second = second[:C] + second[C:] + dot_nn(a_high, low)
+        gate_sum = (git[:, cols] - bt[:, cols] * second).astype(BF)
+        for k in range(n_pb // 2):
+            dgi[part * (n_pb // 2) + k] = gate_sum[:, k * i_rows:(k + 1) * i_rows]
+
+    def item_sends(first, last):
+        sent = []
+        for k in range(first, last):
+            sent.append(send(di.at[i_at(others[k])], item_q.at[k], (ri_send.at[k, 0], ri_recv.at[k, 0]), (others[k], j)))
+            sent.append(send(dgi.at[others[k]], item_g.at[k], (ri_send.at[k, 1], ri_recv.at[k, 1]), (others[k], j)))
+        return sent
+
+    side = p // (n_pb // 2)
+    item_half(1 - side)
+    item_copies = item_sends(0, n_pb // 2)
     far = []
     for k, peer in enumerate(peers):
         for m, (src, got, staged, dst) in enumerate(((dq, near_q, out_q, far_q), (dgq, near_g, out_g, far_g))):
             near[k + 1][m].wait_recv()
             staged[k] = (src[q_at(peer), :].astype(F32) + got[k + 1].astype(F32)).astype(BF)
             far.append(send(staged.at[k], dst.at[k], (rz_send.at[k, m], rz_recv.at[k, m]), (p, peer)))
-    pl.loop(KQ // 4, KQ)(item_step)
-
-    di[...] = dot_nt(eye_i, dit[...].astype(BF)).astype(BF)
-    item_copies = [send(di.at[i_at(row)], item_q.at[k], (ri_send.at[k, 0], ri_recv.at[k, 0]), (row, j))
-                   for k, row in enumerate(others)]
-    i_second = dot_nn(jnp.concatenate([a_high, a_low], axis=0), v_high)
-    i_second = i_second[:C] + i_second[C:] + dot_nn(a_high, v_low)
-    gate_sum = (git[...] - bt[...] * i_second).astype(BF)
-    for k in range(n_pb):
-        dgi[k] = gate_sum[:, k * i_rows:(k + 1) * i_rows]
-    item_copies += [send(dgi.at[row], item_g.at[k], (ri_send.at[k, 1], ri_recv.at[k, 1]), (row, j))
-                    for k, row in enumerate(others)]
+    item_half(side)
+    item_copies += item_sends(n_pb // 2, n_pb - 1)
 
     for copy in near[0] + far:
         copy.wait_recv()

time: 48.1 us -> 44.7 us (0.929)
  local copies, waits for them, and re-layouts: 7.27 us -> 4.26 us
    unnamed x16 -> x8, local copies, waits for them, and re-layouts: 7.27 us -> 4.26 us
where the time goes in v3:
time: 44.7 us; the launch traced here: 44.4 us
  Pallas kernels  39.5 us (88%)
  local copies, waits for them, and re-layouts  4.26 us (10%)
  between operations  0.65 us (1%)
    pallas_call x1, Pallas kernels, on_device(): pl.pallas_call(functools.partial(kernel, n_pb, n_item), out_shape=(jax.Sh...  39.5 us
    unnamed x8, local copies, waits for them, and re-layouts  4.26 us

profile of v3, /device:TPU:0, one launch (start us, length us, event | category | flops | bytes accessed | tf_op | source)
XLA Modules:
  0.0 44.4 jit_solution(10835378441941420714)
XLA Ops:
  0.6 39.5 %scoring_backward.1 = (bf16[64,512]{1,0:T(8,128)(2,1)}, f32[64,64]{1,0:T(8,128)}, bf16[128,512]{1,0:T(8,128)(2,1)}, f32[64,128]{1,0:T(8,128)}) custom-call(s32[1,6]{1,0:T(1,128)} %tiles.1, bf16[64,512]{1,0:T(8,128)(2,1)} %q_ref.1, bf16[64,64]{1,0:T(8,128)(2,1)} %gq_ref.1, bf16[128,512]{1,0:T(8,128)(2,1)} %i_ref.1, bf16[64,128]{1,0:T(8,128)(2,1)} %bitcast.5, ...), custom_call_target="tpu_custom_call" | custom-call | tf_op jit(solution)/shard_map/scoring_backward/pallas_call | solution.py:280
  40.2 0.0 copy-start
  40.2 1.5 %copy.14 = bf16[64,512]{1,0:T(8,128)(2,1)} copy(bf16[64,512]{1,0:T(8,128)(2,1)} %get-tuple-element.16) | data formatting | bytes 131072
  41.7 1.4 %copy.15 = f32[64,64]{1,0:T(8,128)} copy(f32[64,64]{1,0:T(8,128)} %get-tuple-element.17) | data formatting | bytes 32768
  43.1 0.0 copy-done
  43.1 0.0 copy-start.1
  43.1 0.7 %copy.16 = bf16[128,512]{1,0:T(8,128)(2,1)} copy(bf16[128,512]{1,0:T(8,128)(2,1)S(1)} %copy-done) | data formatting | bytes 262144
  43.7 0.1 copy-done.1
  43.8 0.6 %copy.17 = f32[128,64]{0,1:T(8,128)} copy(f32[128,64]{0,1:T(8,128)S(1)} %bitcast.4) | data formatting | bytes 65536
Async XLA Ops:
  40.2 2.9 %copy-start = (bf16[128,512]{1,0:T(8,128)(2,1)S(1)}, bf16[128,512]{1,0:T(8,128)(2,1)}, u32[]{:S(2)}) copy-start(bf16[128,512]{1,0:T(8,128)(2,1)} %get-tuple-element.18) | copy-start | bytes 393220
  43.1 0.8 %copy-start.1 = (f32[64,128]{1,0:T(8,128)S(1)}, f32[64,128]{1,0:T(8,128)}, u32[]{:S(2)}) copy-start(f32[64,128]{1,0:T(8,128)} %get-tuple-element.11) | copy-start | bytes 98308

commit v4 on v3

--- a/solution.py
+++ b/solution.py
@@ -14,7 +14,7 @@
 MESH = pl.DeviceIdType.MESH
 BF = jnp.bfloat16
 F32 = jnp.float32
-VMEM_BYTES = 64 * 1024 * 1024
+VMEM_BYTES = 48 * 1024 * 1024
 
 
 def dot_nn(x, y):
@@ -105,13 +105,21 @@
         copy.start()
     s[...] = jnp.zeros_like(s)
     dit[...] = jnp.zeros_like(dit)
+    local[4].wait()
+    for qb in range(nq // extent):
+        for ib in range(item_blocks):
+            tile_id = qb * item_blocks + ib
+            t = jnp.zeros((extent, extent), F32)
+            for slot in range(slots):
+                t = jnp.where(tiles[0, slot] == tile_id, d_ref[slot].astype(F32), t)
+            v[qb * extent:(qb + 1) * extent, ib * extent:(ib + 1) * extent] = t
     for k in range(len(peers)):
         source = lax.rem(j + n_item - 2 * (k + 1), n_item)
         for m, dst in enumerate((bq, bgq)):
             arrivals[k][m].wait_recv()
             copies.append(send(dst.at[q_at(source)], dst.at[q_at(source)],
                                (f_send.at[k + 1, m], f_recv.at[k + 1, m]), (p, sibling)))
-    for copy in local:
+    for copy in local[:4]:
         copy.wait()
     for copy in item_arrivals:
         copy.wait_recv()
@@ -156,12 +164,8 @@
         here = slice(qb * extent, (qb + 1) * extent)
         for ib in range(item_blocks):
             there = slice(ib * extent, (ib + 1) * extent)
-            tile_id = qb * item_blocks + ib
-            t = jnp.zeros((extent, extent), F32)
-            for slot in range(slots):
-                t = jnp.where(tiles[0, slot] == tile_id, d_ref[slot].astype(F32), t)
             scale = 1.0 / total[here, there]
-            rounded = (t * scale).astype(BF)
+            rounded = (v[here, there] * scale).astype(BF)
             u[here, there] = rounded
             v[here, there] = rounded.astype(F32) * (s[here, there] * scale)
 
@@ -268,7 +272,7 @@
     half = n_item // 2
     peers, others = max(half - 1, 1), max(n_pb - 1, 1)
     vmem = pl.BlockSpec(memory_space=pltpu.VMEM)
-    hbm = pl.BlockSpec(memory_space=pl.ANY)
+    hbm = pl.BlockSpec(memory_space=pltpu.HBM)
     scratch = [((nq, width), BF), ((nq, C), BF), ((ni, width), BF), ((n_pb, C, i_rows), BF), (cotangents.shape, BF),
                ((width, nq), F32), ((width, ni), F32), ((C, nq), F32), ((C, ni), F32),
                ((C * E, nq), BF), ((C * E, ni), BF), ((nq, ni), F32), ((nq, ni), BF), ((nq, ni), F32),
@@ -287,7 +291,8 @@
         + [pltpu.SemaphoreType.DMA(shape) for shape in sems],
         compiler_params=pltpu.CompilerParams(collective_id=0, has_side_effects=True, vmem_limit_bytes=VMEM_BYTES),
         name="scoring_backward",
-    )(slot_tiles, queries, gate_query, items, gate_items.T, cotangents)
+    )(slot_tiles, *[pltpu.with_memory_space_constraint(x, pltpu.HBM)
+                    for x in (queries, gate_query, items, gate_items.T, cotangents)])
     return out[0], out[1], out[2], out[3].T
 
 

time: 44.7 us -> 42.4 us (0.949)
  Pallas kernels: 39.5 us -> 38.4 us
  local copies, waits for them, and re-layouts: 4.26 us -> 3.16 us
    pallas_call x1, Pallas kernels: 39.5 us -> 38.4 us  [on_device(): pl.pallas_call(functools.partial(kernel, n_pb, n_item), out_shape=(jax.Sh...]
    unnamed x8 -> x6, local copies, waits for them, and re-layouts: 4.26 us -> 3.16 us
where the time goes in v4:
time: 42.4 us; the launch traced here: 42.2 us
  Pallas kernels  38.4 us (91%)
  local copies, waits for them, and re-layouts  3.16 us (7%)
  between operations  0.65 us (2%)
    pallas_call x1, Pallas kernels, on_device(): pl.pallas_call(functools.partial(kernel, n_pb, n_item), out_shape=(jax.Sh...  38.4 us
    unnamed x6, local copies, waits for them, and re-layouts  3.16 us

profile of v4, /device:TPU:0, one launch (start us, length us, event | category | flops | bytes accessed | tf_op | source)
XLA Modules:
  0.0 42.2 jit_solution(8400120793750161327)
XLA Ops:
  0.6 0.0 copy-start
  0.6 0.6 %copy-done = s32[1,6]{1,0:T(1,128)S(1)} copy-done((s32[1,6]{1,0:T(1,128)S(1)}, s32[1,6]{1,0:T(1,128)}, u32[]{:S(2)}) %copy-start) | copy-done | bytes 48
  1.3 38.4 %scoring_backward.1 = (bf16[64,512]{1,0:T(8,128)(2,1)S(1)}, f32[64,64]{1,0:T(8,128)S(1)}, bf16[128,512]{1,0:T(8,128)(2,1)S(1)}, f32[64,128]{1,0:T(8,128)S(1)}) custom-call(s32[1,6]{1,0:T(1,128)S(1)} %copy-done, bf16[64,512]{1,0:T(8,128)(2,1)} %q_ref.1, bf16[64,64]{1,0:T(8,128)(2,1)} %gq_ref.1, bf16[128,512]{1,0:T(8,128)(2,1)} %i_ref.1, ...), custom_call_target="tpu_custom_call" | custom-call | tf_op jit(solution)/shard_map/scoring_backward/pallas_call | solution.py:284
  39.7 0.6 %copy.14 = bf16[64,512]{1,0:T(8,128)(2,1)} copy(bf16[64,512]{1,0:T(8,128)(2,1)S(1)} %get-tuple-element.16) | data formatting | bytes 131072
  40.3 0.6 %copy.15 = f32[64,64]{1,0:T(8,128)} copy(f32[64,64]{1,0:T(8,128)S(1)} %get-tuple-element.17) | data formatting | bytes 32768
  41.0 0.7 %copy.16 = bf16[128,512]{1,0:T(8,128)(2,1)} copy(bf16[128,512]{1,0:T(8,128)(2,1)S(1)} %get-tuple-element.18) | data formatting | bytes 262144
  41.6 0.6 %copy.17 = f32[128,64]{0,1:T(8,128)} copy(f32[128,64]{0,1:T(8,128)S(1)} %bitcast.3) | data formatting | bytes 65536
Async XLA Ops:
  0.6 0.7 %copy-start = (s32[1,6]{1,0:T(1,128)S(1)}, s32[1,6]{1,0:T(1,128)}, u32[]{:S(2)}) copy-start(s32[1,6]{1,0:T(1,128)} %tiles.1) | copy-start | bytes 76
